TPU v7x, 256 devices: a whole 4x4x8 slice. The times are simulated.
256 devices in a mesh: lat: 64 (over x, z, core), head: 4 (over y).
Axes of the slice: x: 4, y: 4, z: 8, core: 2. Of those that a mesh axis runs over, the one named last changes fastest.
Arguments:
- level_tokens: bfloat16 [32768, 13, 1024], P('lat'), may hold values from -400 to 400
- ln_gain: float32 [1024], replicated, may hold values from 0.25 to 1.75
- key_weight: bfloat16 [1024, 1024], P(None, 'head'), may hold values from -0.1875 to 0.1875
- value_weight: bfloat16 [1024, 1024], P(None, 'head'), may hold values from -0.1875 to 0.1875
- out_weight: bfloat16 [1024, 1024], P('head'), may hold values from -0.1875 to 0.1875
- ocean_queries: bfloat16 [32768, 4, 1024], P('lat', None, 'head'), may hold values from -600 to 600
- send_slots: int32 [64, 64, 8], P('lat'), may hold values from -1 to 511, as said below
Outputs:
- ocean_out: bfloat16 [32768, 4, 1024], P('lat', None, 'head')
Inputs may be any that keep to these rules, and one draw needn't show every extreme that they name: `send_slots`: entry [h, o, k] is a patch index within stripe h, or -1 for an empty slot. The live entries of one stripe are distinct, and in each [h, o] row the live entries come first. In every draw some owner has all 8 slots of every stripe live.
All inputs are finite; a program needn't handle non-finite values.
Results may differ from a plain program's by a relative error of at most 0.013.
The roundings to bfloat16 on the way count: a program that leaves them out, or rounds other values in their place, can miss the bound.
Values may be sent and summed in bfloat16 or wider, within the bound.
A program may use at most 128 MiB of HBM per device.

v0:
```python
import math

import jax
import jax.numpy as jnp
from jax import lax
from jax.sharding import PartitionSpec as P

HEAD_DIM = 64


def normalize(rows, gain):
    value_matrix = rows.astype(jnp.float32)
    center = jnp.mean(value_matrix, axis=-1, keepdims=True)
    shifted = value_matrix - center
    spread = jnp.mean(shifted * shifted, axis=-1, keepdims=True)
    return (shifted * lax.rsqrt(spread + 1e-05) * gain).astype(jnp.bfloat16)


def shards(level_tokens, ln_gain, key_weight, value_weight, out_weight, ocean_queries, send_slots):
    heads = lax.axis_size("head")
    patches, levels, feature_width = level_tokens.shape
    slot_count, latents, local_width = ocean_queries.shape
    head_count = local_width // HEAD_DIM
    arrived = lax.all_to_all(ocean_queries, "lat", split_axis=0, concat_axis=0, tiled=True)
    full_out_weight = lax.all_gather(out_weight, "head", axis=0, tiled=True)
    chosen = send_slots.reshape(-1)
    pick = (chosen[:, None] == jnp.arange(patches, dtype=jnp.int32)[None, :]).astype(jnp.bfloat16)
    normed = normalize(level_tokens, ln_gain)
    key_rows = jnp.einsum("pld,de->ple", normed, key_weight, preferred_element_type=jnp.float32).astype(jnp.bfloat16)
    value_rows = jnp.einsum("pld,de->ple", normed, value_weight, preferred_element_type=jnp.float32).astype(jnp.bfloat16)
    key_rows = key_rows.reshape(patches, levels, head_count, HEAD_DIM)
    value_rows = value_rows.reshape(patches, levels, head_count, HEAD_DIM)
    queries = jnp.einsum("sp,sc->pc", pick, arrived.reshape(slot_count, -1), preferred_element_type=jnp.float32).astype(jnp.bfloat16)
    queries = queries.reshape(patches, latents, head_count, HEAD_DIM)
    scores = jnp.einsum("sqhe,slhe->shql", queries, key_rows, preferred_element_type=jnp.float32) / math.sqrt(HEAD_DIM)
    highest = jnp.max(scores, axis=-1, keepdims=True)
    expo = jnp.exp(scores - highest)
    soft = (expo / jnp.sum(expo, axis=-1, keepdims=True)).astype(jnp.bfloat16)
    mixed = jnp.einsum("shql,slhe->sqhe", soft, value_rows, preferred_element_type=jnp.float32).astype(jnp.bfloat16)
    mixed = jnp.einsum("sp,pc->sc", pick, mixed.reshape(patches, latents * local_width), preferred_element_type=jnp.float32).astype(jnp.bfloat16)
    rows = slot_count // heads
    mixed = mixed.reshape(heads, rows * latents, local_width)
    mixed = lax.all_to_all(mixed, "head", split_axis=0, concat_axis=0, tiled=True)
    terms = jnp.einsum("gre,ged->grd", mixed, full_out_weight.reshape(heads, local_width, feature_width), preferred_element_type=jnp.float32).astype(jnp.bfloat16)
    terms = lax.optimization_barrier(terms)
    summed = jnp.sum(terms.astype(jnp.float32), axis=0).astype(jnp.bfloat16)
    summed = summed.reshape(rows * latents, heads, local_width).swapaxes(0, 1)
    summed = lax.all_to_all(summed, "head", split_axis=0, concat_axis=0, tiled=True)
    summed = summed.reshape(slot_count, latents, local_width)
    return lax.all_to_all(summed, "lat", split_axis=0, concat_axis=0, tiled=True)


def solution(mesh):
    return jax.shard_map(
        shards,
        mesh=mesh,
        in_specs=(
            P("lat", None, None),
            P(),
            P(None, "head"),
            P(None, "head"),
            P("head", None),
            P("lat", None, "head"),
            P("lat", None, None),
        ),
        out_specs=P("lat", None, "head"),
        check_vma=False,
    )
```

profile of v0, /device:TPU:1, one launch (start us, length us, event | category | flops | bytes accessed | tf_op | source)
XLA Modules:
  0.0 202.3 jit_solution(6567581599151941485)
XLA Ops:
  6.5 0.0 copy-start
  6.5 13.1 %all-to-all-start = ((bf16[512,4,256]{2,1,0:T(4,128)(2,1)}), bf16[512,4,256]{2,1,0:T(4,128)(2,1)S(1)}, u32[]{:S(2)}, u32[]{:S(2)}) async-start(bf16[512,4,256]{2,1,0:T(4,128)(2,1)} %param.12), calls=%async_computation | async-start | bytes 2097152 | tf_op jit(solution)/shard_map/all_to_all | solution.py:24
  19.7 0.0 all-gather.2.cloned.1.call-start
  19.7 0.7 all-gather.2.cloned.1.call-update
  20.4 6.7 %convert_reduce_fusion = f32[512,13]{0,1:T(8,128)S(1)} fusion(bf16[512,13,1024]{2,0,1:T(8,128)(2,1)} %param.7), kind=kLoop, calls=%fused_computation.2 | loop fusion | flops 13624832 | bytes 13658112 | tf_op jit(solution)/shard_map/reduce_sum | solution.py:13
  27.1 0.0 copy-start.4
  27.2 8.6 %fusion.3 = f32[512,13]{0,1:T(8,128)S(1)} fusion(bf16[512,13,1024]{2,0,1:T(8,128)(2,1)} %param.7, f32[512,13]{0,1:T(8,128)S(1)} %broadcast_multiply_fusion), kind=kLoop, calls=%fused_computation.5 | loop fusion | flops 27256320 | bytes 13684736 | tf_op jit(solution)/shard_map/reduce_sum | solution.py:15
  35.8 0.0 copy-done
  35.8 0.0 copy-done.4
  35.8 10.8 %fusion.16 = bf16[512,13,256]{0,2,1:T(8,128)(2,1)} fusion(bf16[512,13,1024]{2,0,1:T(8,128)(2,1)} %param.7, f32[1024]{0:T(1024)S(1)} %copy-done.4, f32[512,13]{0,1:T(8,128)S(1)} %add_rsqrt_fusion, f32[512,13]{0,1:T(8,128)S(1)} %broadcast_multiply_fusion, bf16[1024,256]{1,0:T(8,128)(2,1)S(1)} %copy-done), kind=kOutput, calls=%fused_computation.16 | convolution fusion | flops 3525443584 | bytes 17620992 | tf_op jit(solution)/shard_map/pld,de->ple/dot_general | solution.py:29
  46.7 0.0 copy-start.2
  46.7 0.0 copy-start.3
  46.7 13.1 %copy.35 = bf16[512,13,4,64]{3,1,2,0:T(8,128)(2,1)} copy(bf16[512,13,4,64]{0,3,2,1:T(8,128)(2,1)} %bitcast.31) | data formatting | bytes 6815744 | tf_op jit(solution)/shard_map/reshape | solution.py:31
  59.7 0.0 copy-done.2
  59.7 0.1 copy.30
  59.8 0.1 eq.15
  59.9 0.0 copy-done.3
  59.9 10.4 %fusion.13 = bf16[512,13,256]{0,2,1:T(8,128)(2,1)} fusion(bf16[512,13,1024]{2,0,1:T(8,128)(2,1)} %param.7, f32[1024]{0:T(1024)S(1)} %copy-done.4, f32[512,13]{0,1:T(8,128)S(1)} %add_rsqrt_fusion, f32[512,13]{0,1:T(8,128)S(1)} %broadcast_multiply_fusion, bf16[1024,256]{1,0:T(8,128)(2,1)S(1)} %copy-done.3), kind=kOutput, calls=%fused_computation.15 | convolution fusion | flops 3525443584 | bytes 17620992 | tf_op jit(solution)/shard_map/pld,de->ple/dot_general | solution.py:30
  70.3 13.0 %copy.36 = bf16[512,13,4,64]{3,1,2,0:T(8,128)(2,1)} copy(bf16[512,13,4,64]{0,3,2,1:T(8,128)(2,1)} %bitcast.30) | data formatting | bytes 6815744 | tf_op jit(solution)/shard_map/reshape | solution.py:32
  83.3 0.0 all-to-all-done
  83.3 0.2 copy.44
  83.5 0.8 convolution_convert_fusion.2
  84.4 0.5 copy.32
  84.9 3.0 %copy.34 = bf16[512,4,4,64]{3,1,2,0:T(4,128)(2,1)} copy(bf16[512,4,4,64]{0,3,2,1:T(8,128)(2,1)S(1)} %bitcast.27) | data formatting | bytes 2097152 | tf_op jit(solution)/shard_map/reshape | solution.py:34
  87.9 10.3 %fusion.27 = (f32[512,4,4]{2,1,0:T(4,128)}, f32[512,4,4,13]{3,2,1,0:T(4,128)}) fusion(bf16[512,4,4,64]{3,1,2,0:T(4,128)(2,1)} %copy.34, bf16[512,13,4,64]{3,1,2,0:T(8,128)(2,1)} %copy.35), kind=kOutput, calls=%fused_computation.31 | convolution fusion | flops 13950988 | bytes 4915200 | tf_op jit(solution)/shard_map/sub | solution.py:37
  98.1 6.4 %convert_bitcast_fusion = bf16[512,4,4,64]{3,1,2,0:T(4,128)(2,1)S(1)} fusion(bf16[512,13,4,64]{3,1,2,0:T(8,128)(2,1)} %copy.36, f32[512,4,4,13]{3,2,1,0:T(4,128)} %get-tuple-element.6, f32[512,4,4]{2,1,0:T(4,128)} %get-tuple-element.5), kind=kOutput, calls=%fused_computation.18 | convolution fusion | flops 14368768 | bytes 4915200 | tf_op jit(solution)/shard_map/shql,slhe->sqhe/dot_general | solution.py:39
  104.5 2.8 %copy.37 = bf16[512,4,4,64]{0,3,2,1:T(8,128)(2,1)} copy(bf16[512,4,4,64]{3,1,2,0:T(4,128)(2,1)S(1)} %convert_bitcast_fusion) | data formatting | bytes 2097152 | tf_op jit(solution)/shard_map/convert_element_type | solution.py:39
  107.3 2.0 convolution_convert_fusion.1
  109.3 0.7 reshape.48
  110.0 18.1 %all_to_all.20 = bf16[4,512,256]{2,1,0:T(8,128)(2,1)S(1)} all-to-all(bf16[4,512,256]{2,1,0:T(8,128)(2,1)S(1)} %reshape.48), channel_id=1, replica_groups=mesh['lat'=64,'head'=4] {'head'}, dimensions={0} | all-to-all | bytes 2097152 | tf_op jit(solution)/shard_map/all_to_all | solution.py:43
  128.1 0.0 all-gather.2.cloned.1.call-done
  128.1 0.0 copy-start.1
  128.1 4.8 %convolution_convert_fusion = bf16[4,512,1024]{2,1,0:T(8,128)(2,1)} fusion(bf16[4,512,256]{2,1,0:T(8,128)(2,1)S(1)} %all_to_all.20, bf16[4,256,1024]{2,1,0:T(8,128)(2,1)} %bitcast.32), kind=kOutput, calls=%fused_computation.14 | convolution fusion | flops 1075838976 | bytes 7340032 | tf_op jit(solution)/shard_map/gre,ged->grd/dot_general | solution.py:44
  132.9 3.3 %reduce_sum.42 = bf16[512,1024]{1,0:T(8,128)(2,1)S(1)} reduce(bf16[4,512,1024]{2,1,0:T(8,128)(2,1)} %convolution_convert_fusion, bf16[]{:T(256)} %constant.14.clone.1), dimensions={0}, to_apply=%region_4.0 | reduce | flops 1572864 | bytes 5242882 | tf_op jit(solution)/shard_map/reduce_sum | solution.py:46
  136.3 0.5 copy.38
  136.8 15.6 %all_to_all.21 = bf16[4,512,256]{1,2,0:T(8,128)(2,1)S(1)} all-to-all(bf16[4,512,256]{1,2,0:T(8,128)(2,1)S(1)} %bitcast.29), channel_id=1, replica_groups=mesh['lat'=64,'head'=4] {'head'}, dimensions={0} | all-to-all | bytes 2097152 | tf_op jit(solution)/shard_map/all_to_all | solution.py:48
  152.5 0.5 copy.39
  153.0 0.3 reshape.51
  153.3 41.2 %all_to_all.22 = bf16[512,4,256]{2,1,0:T(4,128)(2,1)S(1)} all-to-all(bf16[512,4,256]{2,1,0:T(4,128)(2,1)S(1)} %reshape.51), channel_id=1, replica_groups=mesh['lat'=64,'head'=4] {'lat'}, dimensions={0} | all-to-all | bytes 2097152 | tf_op jit(solution)/shard_map/all_to_all | solution.py:50
  194.5 1.0 copy.46
  195.5 0.0 copy-done.1
  (2 shorter events, 0.0 us)
Async XLA Ops:
  6.5 29.3 %copy-start = (bf16[1024,256]{1,0:T(8,128)(2,1)S(1)}, bf16[1024,256]{1,0:T(8,128)(2,1)}, u32[]{:S(2)}) copy-start(bf16[1024,256]{1,0:T(8,128)(2,1)} %param.9) | copy-start | bytes 1572868
  6.5 76.8 %all-to-all-start = ((bf16[512,4,256]{2,1,0:T(4,128)(2,1)}), bf16[512,4,256]{2,1,0:T(4,128)(2,1)S(1)}, u32[]{:S(2)}, u32[]{:S(2)}) async-start(bf16[512,4,256]{2,1,0:T(4,128)(2,1)} %param.12), calls=%async_computation | async-start | bytes 2097152 | tf_op jit(solution)/shard_map/all_to_all | solution.py:24
  19.7 108.4 %all-gather.2.cloned.1.call-start = ((), (), s32[]{:S(2)}) async-start(), calls=%async_computation.4 | async-start | bytes 2621440 | tf_op jit(solution)/shard_map/all_gather | solution.py:25
  27.1 8.7 %copy-start.4 = (f32[1024]{0:T(1024)S(1)}, f32[1024]{0:T(1024)}, u32[]{:S(2)}) copy-start(f32[1024]{0:T(1024)} %param.8) | copy-start | bytes 12292
  46.7 13.1 %copy-start.2 = (s32[1,64,8]{1,2,0:T(8,128)S(1)}, s32[1,64,8]{1,2,0:T(8,128)}, u32[]{:S(2)}) copy-start(s32[1,64,8]{1,2,0:T(8,128)} %param.13) | copy-start | bytes 6148
  46.7 13.3 %copy-start.3 = (bf16[1024,256]{1,0:T(8,128)(2,1)S(1)}, bf16[1024,256]{1,0:T(8,128)(2,1)}, u32[]{:S(2)}) copy-start(bf16[1024,256]{1,0:T(8,128)(2,1)} %param.10) | copy-start | bytes 1572868
  128.1 67.4 %copy-start.1 = (bf16[1024,256]{1,0:T(8,128)(2,1)S(1)}, bf16[1024,256]{1,0:T(8,128)(2,1)}, u32[]{:S(2)}) copy-start(bf16[1024,256]{1,0:T(8,128)(2,1)} %param.9) | copy-start | bytes 1572868
Sparse Core Ops, SparseCore 0:
  22.3 34.5 all-gather.1
where the time goes:
time: 203 us; the launch traced here: 202 us
  blocking collectives  75 us (37%)
  matrix products  45.5 us (22%)
  local copies, waits for them, and re-layouts  35.7 us (18%)
  other arithmetic  18.7 us (9%)
  between operations  13.5 us (7%)
  starting transfers between devices  13.2 us (7%)
    all_to_all x1, blocking collectives, shards(): lax.all_to_all(summed, 'lat', split_axis=0, concat_axis=0, tiled=True)  41.2 us
    all_to_all x1, blocking collectives, shards(): lax.all_to_all(mixed, 'head', split_axis=0, concat_axis=0, tiled=True)  18.1 us
    all_to_all x1, blocking collectives, shards(): lax.all_to_all(summed, 'head', split_axis=0, concat_axis=0, tiled=True)  15.6 us
    all_to_all x1, starting transfers between devices, shards(): lax.all_to_all(ocean_queries, 'lat', split_axis=0, concat_axis=0, tiled=T...  13.1 us
    reshape x1, local copies, waits for them, and re-layouts, shards(): key_rows = key_rows.reshape(patches, levels, head_count, HEAD_DIM)  13.1 us
    reshape x1, local copies, waits for them, and re-layouts, shards(): value_rows = value_rows.reshape(patches, levels, head_count, HEAD_DIM)  13 us
    dot_general x1, matrix products, shards(): jnp.einsum('pld,de->ple', normed, key_weight, preferred_element_type=jnp....  10.8 us
    dot_general x1, matrix products, shards(): jnp.einsum('pld,de->ple', normed, value_weight, preferred_element_type=jn...  10.4 us
  transfers between devices with their start and end apart: 2, of which 0 were waited for; matrix products, arithmetic and copies ran while one was open for 44% of the time, Pallas kernels for 0%

commit v1 on v0

v1 whole, which is shorter than its diff:
```python
import functools
import math

import jax
import jax.numpy as jnp
from jax import lax
from jax.experimental import pallas as pl
from jax.experimental.pallas import tpu as pltpu
from jax.sharding import PartitionSpec as P

HEAD_DIM = 64
CORES = 2
ROWS = 32
MESH = pl.DeviceIdType.MESH


def attend_kernel(
    dims,
    index_ref,
    token_ref,
    gain_ref,
    key_weight_ref,
    value_weight_ref,
    out_weight_ref,
    query_ref,
    out_ref,
    token_buf,
    normed,
    pick,
    keys,
    values,
    query_buf,
    mix_send,
    mix_recv,
    weight_buf,
    out_stage,
    token_sem,
    query_send_sem,
    query_recv_sem,
    mix_send_sem,
    mix_recv_sem,
    weight_send_sem,
    weight_recv_sem,
    out_send_sem,
    out_recv_sem,
):
    nx, nz, ny, caps, latents = dims
    levels, patches, width = token_ref.shape
    local_width = key_weight_ref.shape[1]
    head_count = local_width // HEAD_DIM
    peers = nx * nz * CORES
    high = nz // ny
    block = caps * latents
    share = high * CORES * block
    chunk = nz * CORES * block
    me, my_head = lax.axis_index("lat"), lax.axis_index("head")
    my_x = lax.div(me, nz * CORES)
    my_z = lax.rem(lax.div(me, CORES), nz)
    my_core = lax.rem(me, CORES)

    def offset(dx, place):
        head = lax.div(place, high * CORES)
        upper = lax.rem(lax.div(place, CORES), high)
        return lax.rem(head + dx, ny) + ny * upper, lax.rem(place, CORES)

    def ahead(dx, dz, dc):
        return (lax.rem(my_x + dx, nx) * nz + lax.rem(my_z + dz, nz)) * CORES + lax.rem(my_core + dc, CORES)

    def behind(dx, dz, dc):
        return (lax.rem(my_x - dx + nx, nx) * nz + lax.rem(my_z - dz + nz, nz)) * CORES + lax.rem(
            my_core + dc, CORES
        )

    def token_copy(level, slot):
        return pltpu.make_async_copy(token_ref.at[level], token_buf.at[slot], token_sem.at[slot])

    token_copy(0, 0).start()

    barrier = pltpu.get_barrier_semaphore()

    def greet(head, dx, place):
        dz, dc = offset(dx, place)
        pl.semaphore_signal(barrier, inc=1, device_id=(behind(dx, dz, dc), head), device_id_type=MESH)

    for dx in range(nx):

        @pl.loop(1 if dx == 0 else 0, nz * CORES)
        def _(place, dx=dx):
            dz, dc = offset(dx, place)
            pl.semaphore_signal(barrier, inc=1, device_id=(ahead(dx, dz, dc), my_head), device_id_type=MESH)

    for step in range(1, ny):
        head = lax.rem(my_head + step, ny)
        pl.semaphore_signal(barrier, inc=1, device_id=(me, head), device_id_type=MESH)
        for dx in range(nx):

            @pl.loop(0, high * CORES)
            def _(place, dx=dx, head=head):
                greet(head, dx, head * (high * CORES) + place)

    pl.semaphore_wait(barrier, (peers - 1) + (ny - 1) + (ny - 1) * nx * high * CORES)

    own_queries = pltpu.make_async_copy(
        query_ref.at[pl.ds(pl.multiple_of(me * block, block), block)],
        query_buf.at[0, pl.ds(0, block)],
        query_recv_sem.at[0],
    )
    own_queries.start()
    for dx in range(nx):

        @pl.loop(1 if dx == 0 else 0, nz * CORES)
        def _(place, dx=dx):
            dz, dc = offset(dx, place)
            stripe = behind(dx, dz, dc)
            pltpu.make_async_remote_copy(
                src_ref=query_ref.at[pl.ds(pl.multiple_of(stripe * block, block), block)],
                dst_ref=query_buf.at[dx, pl.ds(pl.multiple_of(place * block, block), block)],
                send_sem=query_send_sem,
                recv_sem=query_recv_sem.at[dx],
                device_id=(stripe, my_head),
                device_id_type=MESH,
            ).start()

    def weight_copy(step):
        return pltpu.make_async_remote_copy(
            src_ref=out_weight_ref,
            dst_ref=weight_buf.at[step - 1],
            send_sem=weight_send_sem.at[step - 1],
            recv_sem=weight_recv_sem.at[step - 1],
            device_id=(me, lax.rem(my_head - step + ny, ny)),
            device_id_type=MESH,
        )

    for step in range(1, ny):
        weight_copy(step).start()

    for dx in range(nx):

        @pl.loop(0, nz)
        def _(pair, dx=dx):
            dz, _ = offset(dx, pair * CORES)
            first, second = ahead(dx, dz, 0), ahead(dx, dz, 1)
            index = jnp.concatenate(
                [
                    index_ref[pl.ds(pl.multiple_of(first * caps, caps), caps), :],
                    index_ref[pl.ds(pl.multiple_of(second * caps, caps), caps), :],
                ],
                axis=0,
            )
            lane = lax.broadcasted_iota(jnp.int32, index.shape, 1)
            row = pl.multiple_of((dx * nz + pair) * (CORES * caps), CORES * caps)
            for tile in range(0, patches, 128):
                hit = (index == lane + tile).astype(jnp.float32)
                pick[pl.ds(row, CORES * caps), tile : tile + 128] = hit[:, : min(128, patches - tile)].astype(
                    jnp.bfloat16
                )

    @pl.loop(0, levels)
    def _(level):
        slot = lax.rem(level, 2)
        token_copy(level, slot).wait()

        @pl.when(level + 1 < levels)
        def _():
            token_copy(level + 1, 1 - slot).start()

        @pl.loop(0, patches // ROWS)
        def _(step):
            rows = pl.ds(pl.multiple_of(step * ROWS, ROWS), ROWS)
            raw = token_buf[slot, rows, :].astype(jnp.float32)
            shifted = raw - jnp.sum(raw, axis=1, keepdims=True) * (1.0 / width)
            spread = jnp.sum(shifted * shifted, axis=1, keepdims=True) * (1.0 / width)
            normed[rows, :] = (shifted * lax.rsqrt(spread + 1e-05) * gain_ref[...]).astype(jnp.bfloat16)

        for weight_ref, kept in ((key_weight_ref, keys), (value_weight_ref, values)):
            projected = jnp.dot(normed[...], weight_ref[...], preferred_element_type=jnp.float32)
            kept[level] = jnp.dot(
                pick[...], projected.astype(jnp.bfloat16), preferred_element_type=jnp.float32
            ).astype(jnp.bfloat16)

    group = CORES * caps
    group_rows = group * latents

    def attend(dx):
        whole = query_buf.at[dx]
        pltpu.make_async_copy(whole, whole, query_recv_sem.at[dx]).wait()

        @pl.loop(0, nz)
        def _(pair):
            slots = pl.ds(pl.multiple_of((dx * nz + pair) * group, group), group)
            rows = pl.ds(pl.multiple_of(pair * group_rows, group_rows), group_rows)
            group_keys = keys[:, slots, :].reshape(levels * group, local_width)
            group_values = values[:, slots, :].reshape(levels * group, local_width)
            queries = query_buf[dx, rows, :]
            lane_head = lax.broadcasted_iota(jnp.int32, (1, local_width), 1) // HEAD_DIM
            by_head = jnp.concatenate(
                [queries * (lane_head == h).astype(jnp.float32).astype(jnp.bfloat16) for h in range(head_count)],
                axis=0,
            )
            scores = lax.dot_general(
                group_keys, by_head, (((1,), (1,)), ((), ())), preferred_element_type=jnp.float32
            ).reshape(levels, group, head_count * group_rows)
            highest = jnp.max(scores, axis=0, keepdims=True)
            expo = jnp.exp2((scores - highest) * (math.log2(math.e) / math.sqrt(HEAD_DIM)))
            total = jnp.sum(expo, axis=0)
            shape = (group, head_count * group_rows)
            column_slot = (lax.broadcasted_iota(jnp.int32, shape, 1) % group_rows) // latents
            own = lax.broadcasted_iota(jnp.int32, shape, 0) == column_slot
            share_of = jnp.where(own, 1.0 / total, 0.0)
            soft = (expo * share_of[None]).astype(jnp.bfloat16).reshape(levels * group, head_count * group_rows)
            mixed = lax.dot_general(
                soft, group_values, (((0,), (0,)), ((), ())), preferred_element_type=jnp.float32
            )
            result = mixed[:group_rows]
            for h in range(1, head_count):
                result = jnp.where(lane_head == h, mixed[h * group_rows : (h + 1) * group_rows], result)
            mix_send[dx, rows, :] = result.astype(jnp.bfloat16)

        for step in range(1, ny):
            head = lax.rem(my_head - step + ny, ny)
            pltpu.make_async_remote_copy(
                src_ref=mix_send.at[dx, pl.ds(pl.multiple_of(head * share, share), share)],
                dst_ref=mix_recv.at[dx, step - 1],
                send_sem=mix_send_sem,
                recv_sem=mix_recv_sem.at[dx],
                device_id=(me, head),
                device_id_type=MESH,
            ).start()

    def out_copy(dx, place, head):
        dz, dc = offset(dx, my_head * (high * CORES) + place)
        return pltpu.make_async_remote_copy(
            src_ref=out_stage.at[dx, head, pl.ds(pl.multiple_of(place * block, block), block)],
            dst_ref=out_ref.at[pl.ds(pl.multiple_of(me * block, block), block)],
            send_sem=out_send_sem,
            recv_sem=out_recv_sem,
            device_id=(ahead(dx, dz, dc), head),
            device_id_type=MESH,
        )

    def project(dx):
        whole = mix_recv.at[dx]
        pltpu.make_async_copy(whole, whole, mix_recv_sem.at[dx]).wait()
        if dx == 0:
            for step in range(1, ny):
                weight_copy(step).wait_recv()
        own = mix_send[dx, pl.ds(pl.multiple_of(my_head * share, share), share), :]
        for head in range(ny):
            columns = slice(head * local_width, (head + 1) * local_width)
            term = jnp.dot(own, out_weight_ref[:, columns], preferred_element_type=jnp.float32)
            summed = term.astype(jnp.bfloat16).astype(jnp.float32)
            for step in range(1, ny):
                term = jnp.dot(
                    mix_recv[dx, step - 1], weight_buf[step - 1, :, columns], preferred_element_type=jnp.float32
                )
                summed += term.astype(jnp.bfloat16).astype(jnp.float32)
            out_stage[dx, head] = summed.astype(jnp.bfloat16)
        if dx == 0:

            @pl.when(my_head == 0)
            def _():
                pltpu.make_async_copy(
                    out_stage.at[0, 0, pl.ds(0, block)],
                    out_ref.at[pl.ds(pl.multiple_of(me * block, block), block)],
                    out_recv_sem,
                ).start()

            @pl.when(my_head != 0)
            def _():
                out_copy(0, 0, 0).start()

        @pl.loop(1 if dx == 0 else 0, high * CORES * ny)
        def _(step):
            out_copy(dx, lax.div(step, ny), lax.rem(step, ny)).start()

    for dx in range(nx):
        attend(dx)
        if dx >= 1:
            project(dx - 1)
    project(nx - 1)

    def drain(ref, sem):
        pltpu.make_async_copy(ref, ref, sem).wait()

    drain(query_ref.at[pl.ds(0, (peers - 1) * block)], query_send_sem)
    for step in range(1, ny):
        weight_copy(step).wait_send()
    drain(mix_send.at[:, pl.ds(0, (ny - 1) * share)], mix_send_sem)
    drain(out_ref.at[pl.ds(0, (peers - 1) * block)], out_send_sem)

    @pl.when(my_head != 0)
    def _():
        drain(out_ref.at[pl.ds(0, block)], out_send_sem)

    drain(out_ref, out_recv_sem)


def shards(sizes, level_tokens, ln_gain, key_weight, value_weight, out_weight, ocean_queries, send_slots):
    nx, nz, ny = sizes
    patches, levels, width = level_tokens.shape
    slot_count, latents, local_width = ocean_queries.shape
    caps = send_slots.shape[2]
    block = caps * latents
    share = nz // ny * CORES * block
    chunk = nz * CORES * block
    index = jnp.broadcast_to(send_slots.reshape(slot_count, 1), (slot_count, 128))
    vmem = pl.BlockSpec(memory_space=pltpu.VMEM)
    anywhere = pl.BlockSpec(memory_space=pl.ANY)
    bf16 = jnp.bfloat16
    dma = pltpu.SemaphoreType.DMA
    result = pl.pallas_call(
        functools.partial(attend_kernel, (nx, nz, ny, caps, latents)),
        out_shape=jax.ShapeDtypeStruct((slot_count * latents, local_width), bf16),
        in_specs=[vmem, anywhere, vmem, vmem, vmem, vmem, anywhere],
        out_specs=anywhere,
        scratch_shapes=[
            pltpu.VMEM((2, patches, width), bf16),
            pltpu.VMEM((patches, width), bf16),
            pltpu.VMEM((slot_count, patches), bf16),
            pltpu.VMEM((levels, slot_count, local_width), bf16),
            pltpu.VMEM((levels, slot_count, local_width), bf16),
            pltpu.VMEM((nx, chunk, local_width), bf16),
            pltpu.VMEM((nx, chunk, local_width), bf16),
            pltpu.VMEM((nx, ny - 1, share, local_width), bf16),
            pltpu.VMEM((ny - 1, local_width, width), bf16),
            pltpu.VMEM((nx, ny, share, local_width), bf16),
            dma((2,)),
            dma,
            dma((nx,)),
            dma,
            dma((nx,)),
            dma((ny - 1,)),
            dma((ny - 1,)),
            dma,
            dma,
        ],
        compiler_params=pltpu.CompilerParams(
            collective_id=0, has_side_effects=True, vmem_limit_bytes=48 * 1024 * 1024
        ),
    )(
        index,
        level_tokens.transpose(1, 0, 2),
        ln_gain.reshape(1, width),
        key_weight,
        value_weight,
        out_weight,
        ocean_queries.reshape(slot_count * latents, local_width),
    )
    return result.reshape(slot_count, latents, local_width)


def solution(mesh):
    ny = mesh.shape["head"]
    nz = 2 * ny
    nx = mesh.shape["lat"] // (nz * CORES)
    return jax.shard_map(
        functools.partial(shards, (nx, nz, ny)),
        mesh=mesh,
        in_specs=(
            P("lat", None, None),
            P(),
            P(None, "head"),
            P(None, "head"),
            P("head", None),
            P("lat", None, "head"),
            P("lat", None, None),
        ),
        out_specs=P("lat", None, "head"),
        check_vma=False,
    )
```

time: 203 us -> 128 us (0.63)
  Pallas kernels: 0 us -> 121 us
  blocking collectives: 75 us -> 0 us
  matrix products: 45.5 us -> 0 us
  local copies, waits for them, and re-layouts: 35.7 us -> 7.25 us
  other arithmetic: 18.7 us -> 0 us
  between operations: 13.5 us -> 0.04 us
  starting transfers between devices: 13.2 us -> 0 us
    pallas_call x0 -> x1, Pallas kernels: none -> 121 us  [shards(): pl.pallas_call(functools.partial(attend_kernel, (nx, nz, ny, caps, latent...]
    all_to_all x3 -> x0, blocking collectives: 75 us -> none  [the longest x1 41.2 us: shards(): lax.all_to_all(summed, 'lat', split_axis=0, concat_axis=0, tiled=True)]
    dot_general x6 -> x0, matrix products: 35.2 us -> none  [the longest x1 10.8 us: shards(): jnp.einsum('pld,de->ple', normed, key_weight, preferred_element_type=jnp....]
    reshape x5 -> x2, local copies, waits for them, and re-layouts: 30 us -> 2.46 us  [the longest x1 1.35 us: shards(): ocean_queries.reshape(slot_count * latents, local_width)]
    reduce_sum x3 -> x0, other arithmetic: 18.7 us -> none  [the longest x1 8.63 us: normalize(): spread = jnp.mean(shifted * shifted, axis=-1, keepdims=True)]
    all_to_all x1 -> x0, starting transfers between devices: 13.1 us -> none  [shards(): lax.all_to_all(ocean_queries, 'lat', split_axis=0, concat_axis=0, tiled=T...]
    sub x1 -> x0, matrix products: 10.3 us -> none  [shards(): expo = jnp.exp(scores - highest)]
    convert_element_type x2 -> x0, local copies, waits for them, and re-layouts: 3.31 us -> none  [the longest x1 2.76 us: shards(): jnp.einsum('shql,slhe->sqhe', soft, value_rows, preferred_element_type=jn...]
  transfers between devices with their start and end apart: 2 -> 0, of which waited for: 0 -> 0; matrix products, arithmetic and copies ran while one was open for 44% -> 0% of each run, Pallas kernels for 0% -> 0%
where the time goes in v1:
time: 128 us
  Pallas kernels  121 us (95%)
  local copies, waits for them, and re-layouts  7.25 us (6%)
    pallas_call x1, Pallas kernels, shards(): pl.pallas_call(functools.partial(attend_kernel, (nx, nz, ny, caps, latent...  121 us
    unnamed x9, local copies, waits for them, and re-layouts  4.57 us

profile of v1, /device:TPU:1, one launch (start us, length us, event | category | flops | bytes accessed | tf_op | source)
XLA Modules:
  0.0 128.1 jit_solution(12779369098013614137)
XLA Ops:
  0.0 0.8 copy.8
  0.8 0.1 broadcast_in_dim.7
  0.9 0.1 broadcast_in_dim.8.index_ref
  1.0 1.3 %reshape.12.query_ref = bf16[2048,256]{1,0:T(8,128)(2,1)S(1)} reshape(bf16[512,4,256]{2,1,0:T(4,128)(2,1)} %param.12) | data formatting | bytes 2097152 | tf_op jit(solution)/shard_map/reshape | solution.py:347
  2.4 0.0 copy-start
  2.4 1.0 copy-done
  3.4 0.0 copy-start.1
  3.4 1.0 copy-done.1
  4.4 0.0 copy-start.2
  4.4 1.0 copy-done.2
  5.5 0.0 copy-start.3
  5.5 0.7 copy-done.3
  6.2 120.8 %shard_map.73 = bf16[2048,256]{1,0:T(8,128)(2,1)S(1)} custom-call(s32[512,128]{1,0:T(8,128)S(1)} %broadcast_in_dim.8.index_ref, bf16[13,512,1024]{2,1,0:T(8,128)(2,1)} %bitcast.3, f32[1,1024]{1,0:T(1,128)S(1)} %bitcast.2, bf16[1024,256]{1,0:T(8,128)(2,1)S(1)} %copy-done, bf16[1024,256]{1,0:T(8,128)(2,1)S(1)} %copy-done.1, bf16[256,1024]{1,0:T(8,128)(2,1)S(1)} %copy-done.2, ...), custom_call_target="tpu_custom_call" | custom-call | tf_op jit(solution)/shard_map/pallas_call | solution.py:311
  127.0 1.1 reshape.13
Async XLA Ops:
  2.4 1.0 copy-start
  3.4 1.0 copy-start.1
  4.4 1.0 copy-start.2
  5.5 0.7 copy-start.3

commit v2 on v1

--- a/solution.py
+++ b/solution.py
@@ -25,8 +25,10 @@
     query_ref,
     out_ref,
     token_buf,
+    projection,
     normed,
     pick,
+    projected,
     keys,
     values,
     query_buf,
@@ -35,12 +37,15 @@
     weight_buf,
     out_stage,
     token_sem,
+    projection_sem,
     query_send_sem,
     query_recv_sem,
     mix_send_sem,
     mix_recv_sem,
     weight_send_sem,
     weight_recv_sem,
+    pair_send_sem,
+    pair_recv_sem,
     out_send_sem,
     out_recv_sem,
 ):
@@ -71,10 +76,19 @@
             my_core + dc, CORES
         )
 
-    def token_copy(level, slot):
-        return pltpu.make_async_copy(token_ref.at[level], token_buf.at[slot], token_sem.at[slot])
-
-    token_copy(0, 0).start()
+    def token_copy(level):
+        return pltpu.make_async_copy(token_ref.at[level], token_buf.at[level], token_sem.at[level])
+
+    weight_copies = [
+        pltpu.make_async_copy(ref, projection.at[:, pl.ds(at * local_width, local_width)], projection_sem.at[at])
+        for at, ref in enumerate((key_weight_ref, value_weight_ref))
+    ]
+    own_weight = pltpu.make_async_copy(out_weight_ref, weight_buf.at[0], weight_recv_sem.at[0])
+    for level in range(levels):
+        token_copy(level).start()
+    for copy in weight_copies:
+        copy.start()
+    own_weight.start()
 
     barrier = pltpu.get_barrier_semaphore()
 
@@ -97,6 +111,23 @@
             @pl.loop(0, high * CORES)
             def _(place, dx=dx, head=head):
                 greet(head, dx, head * (high * CORES) + place)
+
+    chosen = index_ref[...].astype(jnp.float32)
+    owner_lane = lax.broadcasted_iota(jnp.int32, chosen.shape, 1)
+    patch = lax.broadcasted_iota(jnp.int32, (caps, patches), 1).astype(jnp.float32)
+
+    def hits(owner):
+        mine = jnp.sum(jnp.where(owner_lane == owner, chosen, 0.0), axis=1, keepdims=True)
+        return (mine == patch).astype(jnp.float32)
+
+    for dx in range(nx):
+
+        @pl.loop(0, nz, unroll=nz)
+        def _(pair, dx=dx):
+            dz, _ = offset(dx, pair * CORES)
+            both = jnp.concatenate([hits(ahead(dx, dz, 0)), hits(ahead(dx, dz, 1))], axis=0)
+            row = pl.multiple_of((dx * nz + pair) * (CORES * caps), CORES * caps)
+            pick[pl.ds(row, CORES * caps), :] = both.astype(jnp.bfloat16)
 
     pl.semaphore_wait(barrier, (peers - 1) + (ny - 1) + (ny - 1) * nx * high * CORES)
 
@@ -121,62 +152,58 @@
                 device_id_type=MESH,
             ).start()
 
+    half = local_width // CORES
+    my_half = pl.ds(pl.multiple_of(my_core * half, half), half)
+
     def weight_copy(step):
         return pltpu.make_async_remote_copy(
-            src_ref=out_weight_ref,
-            dst_ref=weight_buf.at[step - 1],
-            send_sem=weight_send_sem.at[step - 1],
-            recv_sem=weight_recv_sem.at[step - 1],
+            src_ref=out_weight_ref.at[my_half],
+            dst_ref=weight_buf.at[step, my_half],
+            send_sem=weight_send_sem.at[step],
+            recv_sem=weight_recv_sem.at[step],
             device_id=(me, lax.rem(my_head - step + ny, ny)),
             device_id_type=MESH,
         )
 
+    def pair_copy(step):
+        return pltpu.make_async_remote_copy(
+            src_ref=weight_buf.at[step, my_half],
+            dst_ref=weight_buf.at[step, my_half],
+            send_sem=pair_send_sem.at[step],
+            recv_sem=pair_recv_sem.at[step],
+            device_id=(me + 1 - 2 * my_core, my_head),
+            device_id_type=MESH,
+        )
+
     for step in range(1, ny):
         weight_copy(step).start()
 
-    for dx in range(nx):
-
-        @pl.loop(0, nz)
-        def _(pair, dx=dx):
-            dz, _ = offset(dx, pair * CORES)
-            first, second = ahead(dx, dz, 0), ahead(dx, dz, 1)
-            index = jnp.concatenate(
-                [
-                    index_ref[pl.ds(pl.multiple_of(first * caps, caps), caps), :],
-                    index_ref[pl.ds(pl.multiple_of(second * caps, caps), caps), :],
-                ],
-                axis=0,
-            )
-            lane = lax.broadcasted_iota(jnp.int32, index.shape, 1)
-            row = pl.multiple_of((dx * nz + pair) * (CORES * caps), CORES * caps)
-            for tile in range(0, patches, 128):
-                hit = (index == lane + tile).astype(jnp.float32)
-                pick[pl.ds(row, CORES * caps), tile : tile + 128] = hit[:, : min(128, patches - tile)].astype(
-                    jnp.bfloat16
-                )
+    for copy in weight_copies:
+        copy.wait()
 
     @pl.loop(0, levels)
     def _(level):
-        slot = lax.rem(level, 2)
-        token_copy(level, slot).wait()
-
-        @pl.when(level + 1 < levels)
-        def _():
-            token_copy(level + 1, 1 - slot).start()
-
-        @pl.loop(0, patches // ROWS)
+        token_copy(level).wait()
+
+        @pl.loop(0, patches // ROWS, unroll=patches // ROWS)
         def _(step):
             rows = pl.ds(pl.multiple_of(step * ROWS, ROWS), ROWS)
-            raw = token_buf[slot, rows, :].astype(jnp.float32)
+            raw = token_buf[level, rows, :].astype(jnp.float32)
             shifted = raw - jnp.sum(raw, axis=1, keepdims=True) * (1.0 / width)
             spread = jnp.sum(shifted * shifted, axis=1, keepdims=True) * (1.0 / width)
             normed[rows, :] = (shifted * lax.rsqrt(spread + 1e-05) * gain_ref[...]).astype(jnp.bfloat16)
 
-        for weight_ref, kept in ((key_weight_ref, keys), (value_weight_ref, values)):
-            projected = jnp.dot(normed[...], weight_ref[...], preferred_element_type=jnp.float32)
-            kept[level] = jnp.dot(
-                pick[...], projected.astype(jnp.bfloat16), preferred_element_type=jnp.float32
-            ).astype(jnp.bfloat16)
+        projected[...] = jnp.dot(normed[...], projection[...], preferred_element_type=jnp.float32).astype(
+            jnp.bfloat16
+        )
+        ordered = jnp.dot(pick[...], projected[...], preferred_element_type=jnp.float32).astype(jnp.bfloat16)
+        keys[level] = ordered[:, :local_width]
+        values[level] = ordered[:, local_width:]
+
+    own_weight.wait()
+    for step in range(1, ny):
+        weight_copy(step).wait_recv()
+        pair_copy(step).start()
 
     group = CORES * caps
     group_rows = group * latents
@@ -185,7 +212,7 @@
         whole = query_buf.at[dx]
         pltpu.make_async_copy(whole, whole, query_recv_sem.at[dx]).wait()
 
-        @pl.loop(0, nz)
+        @pl.loop(0, nz, unroll=nz)
         def _(pair):
             slots = pl.ds(pl.multiple_of((dx * nz + pair) * group, group), group)
             rows = pl.ds(pl.multiple_of(pair * group_rows, group_rows), group_rows)
@@ -243,15 +270,15 @@
         pltpu.make_async_copy(whole, whole, mix_recv_sem.at[dx]).wait()
         if dx == 0:
             for step in range(1, ny):
-                weight_copy(step).wait_recv()
+                pair_copy(step).wait_recv()
         own = mix_send[dx, pl.ds(pl.multiple_of(my_head * share, share), share), :]
         for head in range(ny):
             columns = slice(head * local_width, (head + 1) * local_width)
-            term = jnp.dot(own, out_weight_ref[:, columns], preferred_element_type=jnp.float32)
+            term = jnp.dot(own, weight_buf[0, :, columns], preferred_element_type=jnp.float32)
             summed = term.astype(jnp.bfloat16).astype(jnp.float32)
             for step in range(1, ny):
                 term = jnp.dot(
-                    mix_recv[dx, step - 1], weight_buf[step - 1, :, columns], preferred_element_type=jnp.float32
+                    mix_recv[dx, step - 1], weight_buf[step, :, columns], preferred_element_type=jnp.float32
                 )
                 summed += term.astype(jnp.bfloat16).astype(jnp.float32)
             out_stage[dx, head] = summed.astype(jnp.bfloat16)
@@ -285,6 +312,7 @@
     drain(query_ref.at[pl.ds(0, (peers - 1) * block)], query_send_sem)
     for step in range(1, ny):
         weight_copy(step).wait_send()
+        pair_copy(step).wait_send()
     drain(mix_send.at[:, pl.ds(0, (ny - 1) * share)], mix_send_sem)
     drain(out_ref.at[pl.ds(0, (peers - 1) * block)], out_send_sem)
 
@@ -303,7 +331,6 @@
     block = caps * latents
     share = nz // ny * CORES * block
     chunk = nz * CORES * block
-    index = jnp.broadcast_to(send_slots.reshape(slot_count, 1), (slot_count, 128))
     vmem = pl.BlockSpec(memory_space=pltpu.VMEM)
     anywhere = pl.BlockSpec(memory_space=pl.ANY)
     bf16 = jnp.bfloat16
@@ -311,34 +338,39 @@
     result = pl.pallas_call(
         functools.partial(attend_kernel, (nx, nz, ny, caps, latents)),
         out_shape=jax.ShapeDtypeStruct((slot_count * latents, local_width), bf16),
-        in_specs=[vmem, anywhere, vmem, vmem, vmem, vmem, anywhere],
+        in_specs=[vmem, anywhere, vmem, anywhere, anywhere, anywhere, anywhere],
         out_specs=anywhere,
         scratch_shapes=[
-            pltpu.VMEM((2, patches, width), bf16),
+            pltpu.VMEM((levels, patches, width), bf16),
+            pltpu.VMEM((width, 2 * local_width), bf16),
             pltpu.VMEM((patches, width), bf16),
             pltpu.VMEM((slot_count, patches), bf16),
+            pltpu.VMEM((patches, 2 * local_width), bf16),
             pltpu.VMEM((levels, slot_count, local_width), bf16),
             pltpu.VMEM((levels, slot_count, local_width), bf16),
             pltpu.VMEM((nx, chunk, local_width), bf16),
             pltpu.VMEM((nx, chunk, local_width), bf16),
             pltpu.VMEM((nx, ny - 1, share, local_width), bf16),
-            pltpu.VMEM((ny - 1, local_width, width), bf16),
+            pltpu.VMEM((ny, local_width, width), bf16),
             pltpu.VMEM((nx, ny, share, local_width), bf16),
+            dma((levels,)),
             dma((2,)),
             dma,
             dma((nx,)),
             dma,
             dma((nx,)),
-            dma((ny - 1,)),
-            dma((ny - 1,)),
+            dma((ny,)),
+            dma((ny,)),
+            dma((ny,)),
+            dma((ny,)),
             dma,
             dma,
         ],
         compiler_params=pltpu.CompilerParams(
-            collective_id=0, has_side_effects=True, vmem_limit_bytes=48 * 1024 * 1024
+            collective_id=0, has_side_effects=True, vmem_limit_bytes=60 * 1024 * 1024
         ),
     )(
-        index,
+        send_slots.reshape(-1, caps).T,
         level_tokens.transpose(1, 0, 2),
         ln_gain.reshape(1, width),
         key_weight,

time: 128 us -> 78.6 us (0.61)
  the two profiles are of different devices: /device:TPU:1 before, /device:TPU:29 now
where the time goes in v2:
time: 78.6 us; the launch traced here: 78.4 us
  Pallas kernels  74.2 us (94%)
  local copies, waits for them, and re-layouts  4.27 us (5%)
    pallas_call x1, Pallas kernels, shards(): pl.pallas_call(functools.partial(attend_kernel, (nx, nz, ny, caps, latent...  74.2 us
    reshape x1, local copies, waits for them, and re-layouts, shards(): return result.reshape(slot_count, latents, local_width)  2.14 us
    reshape x1, local copies, waits for them, and re-layouts, shards(): ocean_queries.reshape(slot_count * latents, local_width)  2.13 us

profile of v2, /device:TPU:29, one launch (start us, length us, event | category | flops | bytes accessed | tf_op | source)
XLA Modules:
  0.0 78.4 jit_solution(6937268660551350338)
XLA Ops:
  0.0 2.1 %reshape.14.query_ref = bf16[2048,256]{1,0:T(8,128)(2,1)} reshape(bf16[512,4,256]{2,1,0:T(4,128)(2,1)} %param.12) | data formatting | bytes 2097152 | tf_op jit(solution)/shard_map/reshape | solution.py:379
  2.1 74.2 %shard_map.73 = bf16[2048,256]{1,0:T(8,128)(2,1)} custom-call(s32[8,64]{1,0:T(8,128)} %bitcast.6, bf16[13,512,1024]{2,1,0:T(8,128)(2,1)} %bitcast.5, f32[1,1024]{1,0:T(1,128)} %bitcast.7, bf16[1024,256]{1,0:T(8,128)(2,1)} %key_weight_ref.1, bf16[1024,256]{1,0:T(8,128)(2,1)} %value_weight_ref.1, bf16[256,1024]{1,0:T(8,128)(2,1)} %out_weight_ref.1, ...), custom_call_target="tpu_custom_call" | custom-call | tf_op jit(solution)/shard_map/pallas_call | solution.py:338
  76.3 2.1 %reshape.15 = bf16[512,4,256]{2,1,0:T(4,128)(2,1)} reshape(bf16[2048,256]{1,0:T(8,128)(2,1)} %shard_map.73) | data formatting | bytes 2097152 | tf_op jit(solution)/shard_map/reshape | solution.py:381

commit v3 on v2

--- a/solution.py
+++ b/solution.py
@@ -10,7 +10,6 @@
 
 HEAD_DIM = 64
 CORES = 2
-ROWS = 32
 MESH = pl.DeviceIdType.MESH
 
 
@@ -28,7 +27,6 @@
     projection,
     normed,
     pick,
-    projected,
     keys,
     values,
     query_buf,
@@ -92,25 +90,21 @@
 
     barrier = pltpu.get_barrier_semaphore()
 
-    def greet(head, dx, place):
-        dz, dc = offset(dx, place)
-        pl.semaphore_signal(barrier, inc=1, device_id=(behind(dx, dz, dc), head), device_id_type=MESH)
-
-    for dx in range(nx):
-
-        @pl.loop(1 if dx == 0 else 0, nz * CORES)
-        def _(place, dx=dx):
-            dz, dc = offset(dx, place)
-            pl.semaphore_signal(barrier, inc=1, device_id=(ahead(dx, dz, dc), my_head), device_id_type=MESH)
+    @pl.loop(1, peers)
+    def _(place):
+        dx = lax.div(place, nz * CORES)
+        dz, dc = offset(dx, lax.rem(place, nz * CORES))
+        pl.semaphore_signal(barrier, inc=1, device_id=(ahead(dx, dz, dc), my_head), device_id_type=MESH)
 
     for step in range(1, ny):
         head = lax.rem(my_head + step, ny)
         pl.semaphore_signal(barrier, inc=1, device_id=(me, head), device_id_type=MESH)
-        for dx in range(nx):
-
-            @pl.loop(0, high * CORES)
-            def _(place, dx=dx, head=head):
-                greet(head, dx, head * (high * CORES) + place)
+
+        @pl.loop(0, nx * high * CORES)
+        def _(place, head=head):
+            dx = lax.div(place, high * CORES)
+            dz, dc = offset(dx, head * (high * CORES) + lax.rem(place, high * CORES))
+            pl.semaphore_signal(barrier, inc=1, device_id=(behind(dx, dz, dc), head), device_id_type=MESH)
 
     chosen = index_ref[...].astype(jnp.float32)
     owner_lane = lax.broadcasted_iota(jnp.int32, chosen.shape, 1)
@@ -120,37 +114,16 @@
         mine = jnp.sum(jnp.where(owner_lane == owner, chosen, 0.0), axis=1, keepdims=True)
         return (mine == patch).astype(jnp.float32)
 
-    for dx in range(nx):
-
+    @pl.loop(0, nx)
+    def _(dx):
         @pl.loop(0, nz, unroll=nz)
-        def _(pair, dx=dx):
+        def _(pair):
             dz, _ = offset(dx, pair * CORES)
             both = jnp.concatenate([hits(ahead(dx, dz, 0)), hits(ahead(dx, dz, 1))], axis=0)
             row = pl.multiple_of((dx * nz + pair) * (CORES * caps), CORES * caps)
             pick[pl.ds(row, CORES * caps), :] = both.astype(jnp.bfloat16)
 
     pl.semaphore_wait(barrier, (peers - 1) + (ny - 1) + (ny - 1) * nx * high * CORES)
-
-    own_queries = pltpu.make_async_copy(
-        query_ref.at[pl.ds(pl.multiple_of(me * block, block), block)],
-        query_buf.at[0, pl.ds(0, block)],
-        query_recv_sem.at[0],
-    )
-    own_queries.start()
-    for dx in range(nx):
-
-        @pl.loop(1 if dx == 0 else 0, nz * CORES)
-        def _(place, dx=dx):
-            dz, dc = offset(dx, place)
-            stripe = behind(dx, dz, dc)
-            pltpu.make_async_remote_copy(
-                src_ref=query_ref.at[pl.ds(pl.multiple_of(stripe * block, block), block)],
-                dst_ref=query_buf.at[dx, pl.ds(pl.multiple_of(place * block, block), block)],
-                send_sem=query_send_sem,
-                recv_sem=query_recv_sem.at[dx],
-                device_id=(stripe, my_head),
-                device_id_type=MESH,
-            ).start()
 
     half = local_width // CORES
     my_half = pl.ds(pl.multiple_of(my_core * half, half), half)
@@ -178,47 +151,74 @@
     for step in range(1, ny):
         weight_copy(step).start()
 
+    own_queries = pltpu.make_async_copy(
+        query_ref.at[pl.ds(pl.multiple_of(me * caps, caps), caps)],
+        query_buf.at[0, pl.ds(0, caps)],
+        query_recv_sem.at[0],
+    )
+    own_queries.start()
+    @pl.loop(1, peers)
+    def _(place):
+        dx, at = lax.div(place, nz * CORES), lax.rem(place, nz * CORES)
+        dz, dc = offset(dx, at)
+        stripe = behind(dx, dz, dc)
+        pltpu.make_async_remote_copy(
+            src_ref=query_ref.at[pl.ds(pl.multiple_of(stripe * caps, caps), caps)],
+            dst_ref=query_buf.at[dx, pl.ds(pl.multiple_of(at * caps, caps), caps)],
+            send_sem=query_send_sem,
+            recv_sem=query_recv_sem.at[dx],
+            device_id=(stripe, my_head),
+            device_id_type=MESH,
+        ).start()
+
     for copy in weight_copies:
         copy.wait()
-
-    @pl.loop(0, levels)
-    def _(level):
+    for level in range(levels):
         token_copy(level).wait()
 
-        @pl.loop(0, patches // ROWS, unroll=patches // ROWS)
-        def _(step):
-            rows = pl.ds(pl.multiple_of(step * ROWS, ROWS), ROWS)
-            raw = token_buf[level, rows, :].astype(jnp.float32)
+    chunk_slots = nz * CORES * caps
+
+    def project_tokens(dx):
+        slots = pl.ds(pl.multiple_of(dx * chunk_slots, chunk_slots), chunk_slots)
+        parity = lax.rem(dx, 2)
+
+        def normalize(level):
+            raw = jnp.dot(pick[slots, :], token_buf[level], preferred_element_type=jnp.float32)
             shifted = raw - jnp.sum(raw, axis=1, keepdims=True) * (1.0 / width)
             spread = jnp.sum(shifted * shifted, axis=1, keepdims=True) * (1.0 / width)
-            normed[rows, :] = (shifted * lax.rsqrt(spread + 1e-05) * gain_ref[...]).astype(jnp.bfloat16)
-
-        projected[...] = jnp.dot(normed[...], projection[...], preferred_element_type=jnp.float32).astype(
-            jnp.bfloat16
-        )
-        ordered = jnp.dot(pick[...], projected[...], preferred_element_type=jnp.float32).astype(jnp.bfloat16)
-        keys[level] = ordered[:, :local_width]
-        values[level] = ordered[:, local_width:]
-
-    own_weight.wait()
-    for step in range(1, ny):
-        weight_copy(step).wait_recv()
-        pair_copy(step).start()
+            return (shifted * lax.rsqrt(spread + 1e-05) * gain_ref[...]).astype(jnp.bfloat16)
+
+        def keep(level, at):
+            both = jnp.dot(normed[at], projection[...], preferred_element_type=jnp.float32).astype(jnp.bfloat16)
+            keys[parity, level] = both[:, :local_width]
+            values[parity, level] = both[:, local_width:]
+
+        normed[0] = normalize(0)
+
+        @pl.loop(0, levels // 2, unroll=levels // 2)
+        def _(pair):
+            for at in range(2):
+                following = normalize(2 * pair + at + 1)
+                keep(2 * pair + at, at)
+                normed[1 - at] = following
+
+        keep(levels - 1, 0)
 
     group = CORES * caps
     group_rows = group * latents
 
     def attend(dx):
+        parity = lax.rem(dx, 2)
         whole = query_buf.at[dx]
         pltpu.make_async_copy(whole, whole, query_recv_sem.at[dx]).wait()
 
         @pl.loop(0, nz, unroll=nz)
         def _(pair):
-            slots = pl.ds(pl.multiple_of((dx * nz + pair) * group, group), group)
+            slots = pl.ds(pl.multiple_of(pair * group, group), group)
             rows = pl.ds(pl.multiple_of(pair * group_rows, group_rows), group_rows)
-            group_keys = keys[:, slots, :].reshape(levels * group, local_width)
-            group_values = values[:, slots, :].reshape(levels * group, local_width)
-            queries = query_buf[dx, rows, :]
+            group_keys = keys[parity, :, slots, :].reshape(levels * group, local_width)
+            group_values = values[parity, :, slots, :].reshape(levels * group, local_width)
+            queries = query_buf[dx, slots].reshape(group_rows, local_width)
             lane_head = lax.broadcasted_iota(jnp.int32, (1, local_width), 1) // HEAD_DIM
             by_head = jnp.concatenate(
                 [queries * (lane_head == h).astype(jnp.float32).astype(jnp.bfloat16) for h in range(head_count)],
@@ -257,8 +257,8 @@
     def out_copy(dx, place, head):
         dz, dc = offset(dx, my_head * (high * CORES) + place)
         return pltpu.make_async_remote_copy(
-            src_ref=out_stage.at[dx, head, pl.ds(pl.multiple_of(place * block, block), block)],
-            dst_ref=out_ref.at[pl.ds(pl.multiple_of(me * block, block), block)],
+            src_ref=out_stage.at[dx, head, pl.ds(pl.multiple_of(place * caps, caps), caps)],
+            dst_ref=out_ref.at[pl.ds(pl.multiple_of(me * caps, caps), caps)],
             send_sem=out_send_sem,
             recv_sem=out_recv_sem,
             device_id=(ahead(dx, dz, dc), head),
@@ -268,9 +268,6 @@
     def project(dx):
         whole = mix_recv.at[dx]
         pltpu.make_async_copy(whole, whole, mix_recv_sem.at[dx]).wait()
-        if dx == 0:
-            for step in range(1, ny):
-                pair_copy(step).wait_recv()
         own = mix_send[dx, pl.ds(pl.multiple_of(my_head * share, share), share), :]
         for head in range(ny):
             columns = slice(head * local_width, (head + 1) * local_width)
@@ -281,44 +278,69 @@
                     mix_recv[dx, step - 1], weight_buf[step, :, columns], preferred_element_type=jnp.float32
                 )
                 summed += term.astype(jnp.bfloat16).astype(jnp.float32)
-            out_stage[dx, head] = summed.astype(jnp.bfloat16)
-        if dx == 0:
-
-            @pl.when(my_head == 0)
-            def _():
-                pltpu.make_async_copy(
-                    out_stage.at[0, 0, pl.ds(0, block)],
-                    out_ref.at[pl.ds(pl.multiple_of(me * block, block), block)],
-                    out_recv_sem,
-                ).start()
-
-            @pl.when(my_head != 0)
-            def _():
-                out_copy(0, 0, 0).start()
-
-        @pl.loop(1 if dx == 0 else 0, high * CORES * ny)
+            out_stage[dx, head] = summed.astype(jnp.bfloat16).reshape(share // latents, latents, local_width)
+        own_place = (dx == 0) & (my_head == 0)
+
+        @pl.when(own_place)
+        def _():
+            pltpu.make_async_copy(
+                out_stage.at[0, 0, pl.ds(0, caps)],
+                out_ref.at[pl.ds(pl.multiple_of(me * caps, caps), caps)],
+                out_recv_sem,
+            ).start()
+
+        @pl.when(jnp.logical_not(own_place))
+        def _():
+            out_copy(dx, 0, 0).start()
+
+        @pl.loop(1, high * CORES * ny)
         def _(step):
             out_copy(dx, lax.div(step, ny), lax.rem(step, ny)).start()
 
-    for dx in range(nx):
-        attend(dx)
-        if dx >= 1:
-            project(dx - 1)
+    @pl.loop(0, nx + 1)
+    def _(step):
+        @pl.when(step < nx)
+        def _():
+            project_tokens(step)
+
+        @pl.when(step >= 1)
+        def _():
+            attend(step - 1)
+
+        @pl.when(step == 1)
+        def _():
+            own_weight.wait()
+            for other in range(1, ny):
+                weight_copy(other).wait_recv()
+                pair_copy(other).start()
+
+        @pl.when(step == 2)
+        def _():
+            for other in range(1, ny):
+                pair_copy(other).wait_recv()
+
+        @pl.when(step >= 2)
+        def _():
+            project(step - 2)
+
+    if nx == 1:
+        for other in range(1, ny):
+            pair_copy(other).wait_recv()
     project(nx - 1)
 
     def drain(ref, sem):
         pltpu.make_async_copy(ref, ref, sem).wait()
 
-    drain(query_ref.at[pl.ds(0, (peers - 1) * block)], query_send_sem)
+    drain(query_ref.at[pl.ds(0, (peers - 1) * caps)], query_send_sem)
     for step in range(1, ny):
         weight_copy(step).wait_send()
         pair_copy(step).wait_send()
     drain(mix_send.at[:, pl.ds(0, (ny - 1) * share)], mix_send_sem)
-    drain(out_ref.at[pl.ds(0, (peers - 1) * block)], out_send_sem)
+    drain(out_ref.at[pl.ds(0, (peers - 1) * caps)], out_send_sem)
 
     @pl.when(my_head != 0)
     def _():
-        drain(out_ref.at[pl.ds(0, block)], out_send_sem)
+        drain(out_ref.at[pl.ds(0, caps)], out_send_sem)
 
     drain(out_ref, out_recv_sem)
 
@@ -333,26 +355,26 @@
     chunk = nz * CORES * block
     vmem = pl.BlockSpec(memory_space=pltpu.VMEM)
     anywhere = pl.BlockSpec(memory_space=pl.ANY)
+    stay = pl.BlockSpec(memory_space=pltpu.HBM)
     bf16 = jnp.bfloat16
     dma = pltpu.SemaphoreType.DMA
-    result = pl.pallas_call(
+    return pl.pallas_call(
         functools.partial(attend_kernel, (nx, nz, ny, caps, latents)),
-        out_shape=jax.ShapeDtypeStruct((slot_count * latents, local_width), bf16),
-        in_specs=[vmem, anywhere, vmem, anywhere, anywhere, anywhere, anywhere],
+        out_shape=jax.ShapeDtypeStruct((slot_count, latents, local_width), bf16),
+        in_specs=[vmem, stay, vmem, stay, stay, stay, anywhere],
         out_specs=anywhere,
         scratch_shapes=[
             pltpu.VMEM((levels, patches, width), bf16),
             pltpu.VMEM((width, 2 * local_width), bf16),
-            pltpu.VMEM((patches, width), bf16),
+            pltpu.VMEM((2, slot_count // nx, width), bf16),
             pltpu.VMEM((slot_count, patches), bf16),
-            pltpu.VMEM((patches, 2 * local_width), bf16),
-            pltpu.VMEM((levels, slot_count, local_width), bf16),
-            pltpu.VMEM((levels, slot_count, local_width), bf16),
-            pltpu.VMEM((nx, chunk, local_width), bf16),
+            pltpu.VMEM((2, levels, slot_count // nx, local_width), bf16),
+            pltpu.VMEM((2, levels, slot_count // nx, local_width), bf16),
+            pltpu.VMEM((nx, chunk // latents, latents, local_width), bf16),
             pltpu.VMEM((nx, chunk, local_width), bf16),
             pltpu.VMEM((nx, ny - 1, share, local_width), bf16),
             pltpu.VMEM((ny, local_width, width), bf16),
-            pltpu.VMEM((nx, ny, share, local_width), bf16),
+            pltpu.VMEM((nx, ny, share // latents, latents, local_width), bf16),
             dma((levels,)),
             dma((2,)),
             dma,
@@ -376,9 +398,8 @@
         key_weight,
         value_weight,
         out_weight,
-        ocean_queries.reshape(slot_count * latents, local_width),
+        ocean_queries,
     )
-    return result.reshape(slot_count, latents, local_width)
 
 
 def solution(mesh):

time: 78.6 us -> 70.4 us (0.90)
  the two profiles are of different devices: /device:TPU:29 before, /device:TPU:1 now
where the time goes in v3:
time: 70.4 us; the launch traced here: 70.1 us
  Pallas kernels  67.5 us (96%)
  local copies, waits for them, and re-layouts  2.56 us (4%)
    pallas_call x1, Pallas kernels, shards(): pl.pallas_call(functools.partial(attend_kernel, (nx, nz, ny, caps, latent...  67.5 us
    unnamed x1, local copies, waits for them, and re-layouts  2.56 us

profile of v3, /device:TPU:1, one launch (start us, length us, event | category | flops | bytes accessed | tf_op | source)
XLA Modules:
  0.0 70.1 jit_solution(14764457886791320267)
XLA Ops:
  0.0 67.5 %shard_map.73 = bf16[512,4,256]{2,1,0:T(4,128)(2,1)} custom-call(s32[8,64]{1,0:T(8,128)} %bitcast.6, bf16[13,512,1024]{2,1,0:T(8,128)(2,1)} %bitcast.5, f32[1,1024]{1,0:T(1,128)} %bitcast.7, bf16[1024,256]{1,0:T(8,128)(2,1)} %key_weight_ref.1, bf16[1024,256]{1,0:T(8,128)(2,1)} %value_weight_ref.1, bf16[256,1024]{1,0:T(8,128)(2,1)} %out_weight_ref.1, ...), custom_call_target="tpu_custom_call" | custom-call | tf_op jit(solution)/shard_map/pallas_call | solution.py:361
  67.5 2.6 %copy.9 = bf16[512,4,256]{2,1,0:T(4,128)(2,1)} copy(bf16[512,4,256]{2,1,0:T(4,128)(2,1)} %shard_map.73) | data formatting | bytes 2097152

commit v4 on v3

--- a/solution.py
+++ b/solution.py
@@ -46,6 +46,8 @@
     pair_recv_sem,
     out_send_sem,
     out_recv_sem,
+    x_ready,
+    heads_ready,
 ):
     nx, nz, ny, caps, latents = dims
     levels, patches, width = token_ref.shape
@@ -90,21 +92,24 @@
 
     barrier = pltpu.get_barrier_semaphore()
 
-    @pl.loop(1, peers)
+    def meet(semaphore, lat, head):
+        pl.semaphore_signal(semaphore, inc=1, device_id=(lat, head), device_id_type=MESH)
+
+    def meet_along_x(semaphore):
+        for dx in range(1, nx):
+            meet(semaphore, ahead(dx, 0, 0), my_head)
+
+    def meet_heads(semaphore):
+        for step in range(1, ny):
+            meet(semaphore, me, lax.rem(my_head + step, ny))
+
+    meet_along_x(barrier)
+    meet_heads(barrier)
+
+    @pl.loop(1, nz * CORES)
     def _(place):
-        dx = lax.div(place, nz * CORES)
-        dz, dc = offset(dx, lax.rem(place, nz * CORES))
-        pl.semaphore_signal(barrier, inc=1, device_id=(ahead(dx, dz, dc), my_head), device_id_type=MESH)
-
-    for step in range(1, ny):
-        head = lax.rem(my_head + step, ny)
-        pl.semaphore_signal(barrier, inc=1, device_id=(me, head), device_id_type=MESH)
-
-        @pl.loop(0, nx * high * CORES)
-        def _(place, head=head):
-            dx = lax.div(place, high * CORES)
-            dz, dc = offset(dx, head * (high * CORES) + lax.rem(place, high * CORES))
-            pl.semaphore_signal(barrier, inc=1, device_id=(behind(dx, dz, dc), head), device_id_type=MESH)
+        dz, dc = offset(0, place)
+        meet(barrier, ahead(0, dz, dc), my_head)
 
     chosen = index_ref[...].astype(jnp.float32)
     owner_lane = lax.broadcasted_iota(jnp.int32, chosen.shape, 1)
@@ -123,7 +128,8 @@
             row = pl.multiple_of((dx * nz + pair) * (CORES * caps), CORES * caps)
             pick[pl.ds(row, CORES * caps), :] = both.astype(jnp.bfloat16)
 
-    pl.semaphore_wait(barrier, (peers - 1) + (ny - 1) + (ny - 1) * nx * high * CORES)
+    pl.semaphore_wait(barrier, (nz * CORES - 1) + (nx - 1) + (ny - 1))
+    meet_along_x(x_ready)
 
     half = local_width // CORES
     my_half = pl.ds(pl.multiple_of(my_core * half, half), half)
@@ -157,8 +163,7 @@
         query_recv_sem.at[0],
     )
     own_queries.start()
-    @pl.loop(1, peers)
-    def _(place):
+    def send_queries(place):
         dx, at = lax.div(place, nz * CORES), lax.rem(place, nz * CORES)
         dz, dc = offset(dx, at)
         stripe = behind(dx, dz, dc)
@@ -170,6 +175,12 @@
             device_id=(stripe, my_head),
             device_id_type=MESH,
         ).start()
+
+    pl.loop(1, nz * CORES)(send_queries)
+    if nx > 1:
+        pl.semaphore_wait(x_ready, nx - 1)
+    meet_heads(heads_ready)
+    pl.loop(nz * CORES, peers)(send_queries)
 
     for copy in weight_copies:
         copy.wait()
@@ -316,6 +327,7 @@
 
         @pl.when(step == 2)
         def _():
+            pl.semaphore_wait(heads_ready, ny - 1)
             for other in range(1, ny):
                 pair_copy(other).wait_recv()
 
@@ -324,6 +336,7 @@
             project(step - 2)
 
     if nx == 1:
+        pl.semaphore_wait(heads_ready, ny - 1)
         for other in range(1, ny):
             pair_copy(other).wait_recv()
     project(nx - 1)
@@ -387,6 +400,8 @@
             dma((ny,)),
             dma,
             dma,
+            pltpu.SemaphoreType.REGULAR,
+            pltpu.SemaphoreType.REGULAR,
         ],
         compiler_params=pltpu.CompilerParams(
             collective_id=0, has_side_effects=True, vmem_limit_bytes=60 * 1024 * 1024

time: 70.4 us -> 67.5 us (0.959)
  Pallas kernels: 67.5 us -> 64.4 us
    pallas_call x1, Pallas kernels: 67.5 us -> 64.4 us  [shards(): pl.pallas_call(functools.partial(attend_kernel, (nx, nz, ny, caps, latent...]
where the time goes in v4:
time: 67.5 us; the launch traced here: 66.9 us
  Pallas kernels  64.4 us (95%)
  local copies, waits for them, and re-layouts  2.56 us (4%)
    pallas_call x1, Pallas kernels, shards(): pl.pallas_call(functools.partial(attend_kernel, (nx, nz, ny, caps, latent...  64.4 us
    unnamed x1, local copies, waits for them, and re-layouts  2.56 us

profile of v4, /device:TPU:1, one launch (start us, length us, event | category | flops | bytes accessed | tf_op | source)
XLA Modules:
  0.0 66.9 jit_solution(13566169555484749254)
XLA Ops:
  0.0 64.4 %shard_map.73 = bf16[512,4,256]{2,1,0:T(4,128)(2,1)} custom-call(s32[8,64]{1,0:T(8,128)} %bitcast.6, bf16[13,512,1024]{2,1,0:T(8,128)(2,1)} %bitcast.5, f32[1,1024]{1,0:T(1,128)} %bitcast.7, bf16[1024,256]{1,0:T(8,128)(2,1)} %key_weight_ref.1, bf16[1024,256]{1,0:T(8,128)(2,1)} %value_weight_ref.1, bf16[256,1024]{1,0:T(8,128)(2,1)} %out_weight_ref.1, ...), custom_call_target="tpu_custom_call" | custom-call | tf_op jit(solution)/shard_map/pallas_call | solution.py:374
  64.4 2.6 %copy.9 = bf16[512,4,256]{2,1,0:T(4,128)(2,1)} copy(bf16[512,4,256]{2,1,0:T(4,128)(2,1)} %shard_map.73) | data formatting | bytes 2097152

commit v5 on v4

--- a/solution.py
+++ b/solution.py
@@ -63,10 +63,9 @@
     my_z = lax.rem(lax.div(me, CORES), nz)
     my_core = lax.rem(me, CORES)
 
-    def offset(dx, place):
-        head = lax.div(place, high * CORES)
-        upper = lax.rem(lax.div(place, CORES), high)
-        return lax.rem(head + dx, ny) + ny * upper, lax.rem(place, CORES)
+    def offset(place):
+        head, at = lax.div(place, high * CORES), lax.rem(place, high * CORES)
+        return (ny // CORES) * at + lax.div(head, CORES), lax.rem(head, CORES)
 
     def ahead(dx, dz, dc):
         return (lax.rem(my_x + dx, nx) * nz + lax.rem(my_z + dz, nz)) * CORES + lax.rem(my_core + dc, CORES)
@@ -108,7 +107,7 @@
 
     @pl.loop(1, nz * CORES)
     def _(place):
-        dz, dc = offset(0, place)
+        dz, dc = offset(place)
         meet(barrier, ahead(0, dz, dc), my_head)
 
     chosen = index_ref[...].astype(jnp.float32)
@@ -123,8 +122,9 @@
     def _(dx):
         @pl.loop(0, nz, unroll=nz)
         def _(pair):
-            dz, _ = offset(dx, pair * CORES)
-            both = jnp.concatenate([hits(ahead(dx, dz, 0)), hits(ahead(dx, dz, 1))], axis=0)
+            both = jnp.concatenate(
+                [hits(ahead(dx, *offset(pair * CORES))), hits(ahead(dx, *offset(pair * CORES + 1)))], axis=0
+            )
             row = pl.multiple_of((dx * nz + pair) * (CORES * caps), CORES * caps)
             pick[pl.ds(row, CORES * caps), :] = both.astype(jnp.bfloat16)
 
@@ -165,7 +165,7 @@
     own_queries.start()
     def send_queries(place):
         dx, at = lax.div(place, nz * CORES), lax.rem(place, nz * CORES)
-        dz, dc = offset(dx, at)
+        dz, dc = offset(at)
         stripe = behind(dx, dz, dc)
         pltpu.make_async_remote_copy(
             src_ref=query_ref.at[pl.ds(pl.multiple_of(stripe * caps, caps), caps)],
@@ -266,7 +266,7 @@
             ).start()
 
     def out_copy(dx, place, head):
-        dz, dc = offset(dx, my_head * (high * CORES) + place)
+        dz, dc = offset(my_head * (high * CORES) + place)
         return pltpu.make_async_remote_copy(
             src_ref=out_stage.at[dx, head, pl.ds(pl.multiple_of(place * caps, caps), caps)],
             dst_ref=out_ref.at[pl.ds(pl.multiple_of(me * caps, caps), caps)],

time: 67.5 us -> 63.4 us (0.939)
  the two profiles are of different devices: /device:TPU:1 before, /device:TPU:26 now
where the time goes in v5:
time: 63.4 us; the launch traced here: 63.3 us
  Pallas kernels  60.7 us (96%)
  local copies, waits for them, and re-layouts  2.56 us (4%)
    pallas_call x1, Pallas kernels, shards(): pl.pallas_call(functools.partial(attend_kernel, (nx, nz, ny, caps, latent...  60.7 us
    unnamed x1, local copies, waits for them, and re-layouts  2.56 us

profile of v5, /device:TPU:26, one launch (start us, length us, event | category | flops | bytes accessed | tf_op | source)
XLA Modules:
  0.0 63.3 jit_solution(17793917530937902005)
XLA Ops:
  0.0 60.7 %shard_map.73 = bf16[512,4,256]{2,1,0:T(4,128)(2,1)} custom-call(s32[8,64]{1,0:T(8,128)} %bitcast.6, bf16[13,512,1024]{2,1,0:T(8,128)(2,1)} %bitcast.5, f32[1,1024]{1,0:T(1,128)} %bitcast.7, bf16[1024,256]{1,0:T(8,128)(2,1)} %key_weight_ref.1, bf16[1024,256]{1,0:T(8,128)(2,1)} %value_weight_ref.1, bf16[256,1024]{1,0:T(8,128)(2,1)} %out_weight_ref.1, ...), custom_call_target="tpu_custom_call" | custom-call | tf_op jit(solution)/shard_map/pallas_call | solution.py:374
  60.7 2.6 %copy.9 = bf16[512,4,256]{2,1,0:T(4,128)(2,1)} copy(bf16[512,4,256]{2,1,0:T(4,128)(2,1)} %shard_map.73) | data formatting | bytes 2097152

commit v6 on v5

--- a/solution.py
+++ b/solution.py
@@ -110,24 +110,6 @@
         dz, dc = offset(place)
         meet(barrier, ahead(0, dz, dc), my_head)
 
-    chosen = index_ref[...].astype(jnp.float32)
-    owner_lane = lax.broadcasted_iota(jnp.int32, chosen.shape, 1)
-    patch = lax.broadcasted_iota(jnp.int32, (caps, patches), 1).astype(jnp.float32)
-
-    def hits(owner):
-        mine = jnp.sum(jnp.where(owner_lane == owner, chosen, 0.0), axis=1, keepdims=True)
-        return (mine == patch).astype(jnp.float32)
-
-    @pl.loop(0, nx)
-    def _(dx):
-        @pl.loop(0, nz, unroll=nz)
-        def _(pair):
-            both = jnp.concatenate(
-                [hits(ahead(dx, *offset(pair * CORES))), hits(ahead(dx, *offset(pair * CORES + 1)))], axis=0
-            )
-            row = pl.multiple_of((dx * nz + pair) * (CORES * caps), CORES * caps)
-            pick[pl.ds(row, CORES * caps), :] = both.astype(jnp.bfloat16)
-
     pl.semaphore_wait(barrier, (nz * CORES - 1) + (nx - 1) + (ny - 1))
     meet_along_x(x_ready)
 
@@ -153,9 +135,6 @@
             device_id=(me + 1 - 2 * my_core, my_head),
             device_id_type=MESH,
         )
-
-    for step in range(1, ny):
-        weight_copy(step).start()
 
     own_queries = pltpu.make_async_copy(
         query_ref.at[pl.ds(pl.multiple_of(me * caps, caps), caps)],
@@ -177,10 +156,31 @@
         ).start()
 
     pl.loop(1, nz * CORES)(send_queries)
+    for step in range(1, ny):
+        weight_copy(step).start()
+
     if nx > 1:
         pl.semaphore_wait(x_ready, nx - 1)
     meet_heads(heads_ready)
     pl.loop(nz * CORES, peers)(send_queries)
+
+    chosen = index_ref[...].astype(jnp.float32)
+    owner_lane = lax.broadcasted_iota(jnp.int32, chosen.shape, 1)
+    patch = lax.broadcasted_iota(jnp.int32, (caps, patches), 1).astype(jnp.float32)
+
+    def hits(owner):
+        mine = jnp.sum(jnp.where(owner_lane == owner, chosen, 0.0), axis=1, keepdims=True)
+        return (mine == patch).astype(jnp.float32)
+
+    @pl.loop(0, nx)
+    def _(dx):
+        @pl.loop(0, nz, unroll=nz)
+        def _(pair):
+            both = jnp.concatenate(
+                [hits(ahead(dx, *offset(pair * CORES))), hits(ahead(dx, *offset(pair * CORES + 1)))], axis=0
+            )
+            row = pl.multiple_of((dx * nz + pair) * (CORES * caps), CORES * caps)
+            pick[pl.ds(row, CORES * caps), :] = both.astype(jnp.bfloat16)
 
     for copy in weight_copies:
         copy.wait()

time: 63.4 us -> 62.7 us (0.989)
  the two profiles are of different devices: /device:TPU:26 before, /device:TPU:1 now
where the time goes in v6:
time: 62.7 us; the launch traced here: 62.1 us
  Pallas kernels  59.5 us (95%)
  local copies, waits for them, and re-layouts  2.56 us (4%)
    pallas_call x1, Pallas kernels, shards(): pl.pallas_call(functools.partial(attend_kernel, (nx, nz, ny, caps, latent...  59.5 us
    unnamed x1, local copies, waits for them, and re-layouts  2.56 us

profile of v6, /device:TPU:1, one launch (start us, length us, event | category | flops | bytes accessed | tf_op | source)
XLA Modules:
  0.0 62.1 jit_solution(6409239870295220597)
XLA Ops:
  0.0 59.5 %shard_map.73 = bf16[512,4,256]{2,1,0:T(4,128)(2,1)} custom-call(s32[8,64]{1,0:T(8,128)} %bitcast.6, bf16[13,512,1024]{2,1,0:T(8,128)(2,1)} %bitcast.5, f32[1,1024]{1,0:T(1,128)} %bitcast.7, bf16[1024,256]{1,0:T(8,128)(2,1)} %key_weight_ref.1, bf16[1024,256]{1,0:T(8,128)(2,1)} %value_weight_ref.1, bf16[256,1024]{1,0:T(8,128)(2,1)} %out_weight_ref.1, ...), custom_call_target="tpu_custom_call" | custom-call | tf_op jit(solution)/shard_map/pallas_call | solution.py:374
  59.5 2.6 %copy.9 = bf16[512,4,256]{2,1,0:T(4,128)(2,1)} copy(bf16[512,4,256]{2,1,0:T(4,128)(2,1)} %shard_map.73) | data formatting | bytes 2097152

commit v7 on v6

--- a/solution.py
+++ b/solution.py
@@ -10,6 +10,7 @@
 
 HEAD_DIM = 64
 CORES = 2
+PIECES = 8
 MESH = pl.DeviceIdType.MESH
 
 
@@ -358,6 +359,20 @@
     drain(out_ref, out_recv_sem)
 
 
+def hand_over_kernel(result_ref, out_ref, held, in_sem, out_sem):
+    rows = result_ref.shape[0] // PIECES
+    pieces = [pl.ds(at * rows, rows) for at in range(PIECES)]
+    arriving = [pltpu.make_async_copy(result_ref.at[p], held.at[p], in_sem.at[at]) for at, p in enumerate(pieces)]
+    leaving = [pltpu.make_async_copy(held.at[p], out_ref.at[p], out_sem.at[at]) for at, p in enumerate(pieces)]
+    for copy in arriving:
+        copy.start()
+    for first, second in zip(arriving, leaving):
+        first.wait()
+        second.start()
+    for copy in leaving:
+        copy.wait()
+
+
 def shards(sizes, level_tokens, ln_gain, key_weight, value_weight, out_weight, ocean_queries, send_slots):
     nx, nz, ny = sizes
     patches, levels, width = level_tokens.shape
@@ -371,7 +386,7 @@
     stay = pl.BlockSpec(memory_space=pltpu.HBM)
     bf16 = jnp.bfloat16
     dma = pltpu.SemaphoreType.DMA
-    return pl.pallas_call(
+    result = pl.pallas_call(
         functools.partial(attend_kernel, (nx, nz, ny, caps, latents)),
         out_shape=jax.ShapeDtypeStruct((slot_count, latents, local_width), bf16),
         in_specs=[vmem, stay, vmem, stay, stay, stay, anywhere],
@@ -415,6 +430,14 @@
         out_weight,
         ocean_queries,
     )
+    return pl.pallas_call(
+        hand_over_kernel,
+        out_shape=jax.ShapeDtypeStruct(result.shape, bf16),
+        in_specs=[anywhere],
+        out_specs=anywhere,
+        scratch_shapes=[pltpu.VMEM(result.shape, bf16), dma((PIECES,)), dma((PIECES,))],
+        compiler_params=pltpu.CompilerParams(vmem_limit_bytes=60 * 1024 * 1024),
+    )(result)
 
 
 def solution(mesh):

time: 62.7 us -> 62.3 us (level)
  local copies, waits for them, and re-layouts: 2.56 us -> 0 us
  Pallas kernels: 59.5 us -> 61.6 us
    unnamed x1 -> x0, local copies, waits for them, and re-layouts: 2.56 us -> none
    pallas_call x0 -> x1, Pallas kernels: none -> 2.09 us  [shards(): pl.pallas_call(hand_over_kernel, out_shape=jax.ShapeDtypeStruct(result.sh...]
where the time goes in v7:
time: 62.3 us; the launch traced here: 61.6 us
  Pallas kernels  61.6 us (99%)
    pallas_call x1, Pallas kernels, shards(): pl.pallas_call(functools.partial(attend_kernel, (nx, nz, ny, caps, latent...  59.5 us
    pallas_call x1, Pallas kernels, shards(): pl.pallas_call(hand_over_kernel, out_shape=jax.ShapeDtypeStruct(result.sh...  2.09 us

profile of v7, /device:TPU:1, one launch (start us, length us, event | category | flops | bytes accessed | tf_op | source)
XLA Modules:
  0.0 61.6 jit_solution(5261380045843681184)
XLA Ops:
  0.0 59.5 %shard_map.73.result_ref = bf16[512,4,256]{2,1,0:T(4,128)(2,1)} custom-call(s32[8,64]{1,0:T(8,128)} %bitcast.6, bf16[13,512,1024]{2,1,0:T(8,128)(2,1)} %bitcast.5, f32[1,1024]{1,0:T(1,128)} %bitcast.7, bf16[1024,256]{1,0:T(8,128)(2,1)} %key_weight_ref.1, bf16[1024,256]{1,0:T(8,128)(2,1)} %value_weight_ref.1, bf16[256,1024]{1,0:T(8,128)(2,1)} %out_weight_ref.1, ...), custom_call_target="tpu_custom_call" | custom-call | tf_op jit(solution)/shard_map/pallas_call | solution.py:389
  59.5 2.1 %shard_map.74 = bf16[512,4,256]{2,1,0:T(4,128)(2,1)} custom-call(bf16[512,4,256]{2,1,0:T(4,128)(2,1)} %shard_map.73.result_ref), custom_call_target="tpu_custom_call" | custom-call | tf_op jit(solution)/shard_map/pallas_call | solution.py:433
